TPU v7x, 32 devices: a whole 2x2x4 slice. The times are simulated.
32 devices in a mesh: tx: 4 (over x, core), ty: 8 (over z, y).
Axes of the slice: x: 2, y: 2, z: 4, core: 2. Of those that a mesh axis runs over, the one named last changes fastest.
Arguments:
- granule_blocks: bfloat16 [2048, 13, 16, 128], P(('tx', 'ty')), may hold values from -6 to 6
- row_weights: bfloat16 [2048, 8, 16], P(('tx', 'ty')), may hold values from -1.5 to 1.5
- column_bank: bfloat16 [8, 128, 128], replicated, may hold values from -0.5 to 0.5
- destination: int32 [2048], P(('tx', 'ty')), may hold values from 0 to 31, as said below
- window_index: int32 [2048], P(('tx', 'ty')), may hold values from 0 to 31
- bank_index: int32 [2048], P(('tx', 'ty')), may hold values from 0 to 7
- kernel_one: bfloat16 [3, 3, 13, 64], replicated, may hold values from -1 to 1
- reduce_two: bfloat16 [2, 2, 64, 128], replicated, may hold values from -0.5 to 0.5
- kernel_two: bfloat16 [3, 3, 128, 128], replicated, may hold values from -0.25 to 0.25
- reduce_three: bfloat16 [2, 2, 128, 256], replicated, may hold values from -0.375 to 0.375
- kernel_three: bfloat16 [3, 3, 256, 256], replicated, may hold values from -0.1875 to 0.1875
- reduce_four: bfloat16 [2, 2, 256, 512], replicated, may hold values from -0.25 to 0.25
- kernel_four: bfloat16 [3, 3, 512, 512], replicated, may hold values from -0.125 to 0.125
Outputs:
- gridded: bfloat16 [13, 2048, 512], P(None, 'ty', 'tx')
- bottleneck: bfloat16 [512, 256, 64], P(None, 'ty', 'tx')
Inputs may be any that keep to these rules, and one draw needn't show every extreme that they name: At most 2 of the blocks that one device holds name the same destination; in every draw one destination is named by 2 blocks of every device.
All inputs are finite; a program needn't handle non-finite values.
Results may differ from a plain program's by a relative error of at most 0.015.
Values may be sent and summed in bfloat16 or wider, within the bound.
No kernel may reach another device: no remote copies, remote signals or barrier semaphores. Data moves between devices by JAX's collectives and lax.ppermute only.
A program may use at most 128 MiB of HBM per device.

v0:
```python
import functools

import jax
import jax.numpy as jnp
import numpy as np
from jax import lax
from jax.experimental import pallas as pl
from jax.experimental.pallas import tpu as pltpu
from jax.sharding import PartitionSpec as P

BF16 = jnp.bfloat16
F32 = jnp.float32
BANDS = 13
SRC_ROWS = 16
WIN_ROWS = 8
CAP = 2
NWIN = 32
TILE_COLS = 128
LINES = BANDS * WIN_ROWS
PACKED = CAP * LINES + WIN_ROWS
STEP_BLOCKS = 8
PHASES = 8
SPOTS = TILE_COLS // PHASES
HALO = 2
WIDE = SPOTS + 2 * HALO
TALL = NWIN + 2 * HALO
POINTS = WIDE * TALL
GROUP = 4
GROUP_POINTS = GROUP * WIDE
VMEM_BYTES = 60 * 1024 * 1024


def dot(a, b):
    return jnp.dot(a, b, preferred_element_type=F32)


def dot_nt(a, b):
    return lax.dot_general(a, b, (((1,), (1,)), ((), ())), preferred_element_type=F32)


def resample_kernel(
    dest_ref, win_ref, choice_ref, weight_ref, raw_ref, bank_ref, spread_ref, mask_ref,
    out_ref, slot_ref, slot_win_ref, held_ref, rows_ref,
):
    step = pl.program_id(0)
    tiles = held_ref.shape[0]

    @pl.when(step == 0)
    def _():
        def clear(i, carry):
            held_ref[i] = 0
            for k in range(CAP):
                slot_win_ref[i * CAP + k] = -1
            return carry

        lax.fori_loop(0, tiles, clear, 0)
        turned = jnp.transpose(weight_ref[...].astype(F32)).astype(BF16)
        blocks = turned.shape[0]
        for r in range(WIN_ROWS):
            wide = dot(turned, spread_ref[r])
            for h in range(2):
                rows_ref[h, pl.ds(r, blocks, stride=WIN_ROWS), :] = wide[:, h * 128:(h + 1) * 128]

    mask = mask_ref[...]
    rowed = []
    for j in range(STEP_BLOCKS):
        row = pl.multiple_of((step * STEP_BLOCKS + j) * WIN_ROWS, WIN_ROWS)
        rows = jnp.concatenate([rows_ref[h, pl.ds(row, WIN_ROWS), :] for h in range(2)], axis=1)
        weights = jnp.concatenate([rows] * BANDS, axis=0) * mask
        weights = weights.astype(BF16)[:, 0:BANDS * SRC_ROWS]
        rowed.append(dot(weights, raw_ref[j]).astype(BF16))
    for j in range(STEP_BLOCKS):
        n = step * STEP_BLOCKS + j
        tile = dest_ref[n]
        rank = held_ref[tile]
        held_ref[tile] = rank + 1
        slot = tile * CAP + rank
        slot_win_ref[slot] = win_ref[n]
        slot_ref[slot] = dot(rowed[j], bank_ref[choice_ref[n]]).astype(BF16)

    @pl.when(step == pl.num_programs(0) - 1)
    def _():
        lane = lax.broadcasted_iota(jnp.int32, (WIN_ROWS, TILE_COLS), 1)

        def pack(i, carry):
            window = jnp.where(lane == 0, slot_win_ref[i * CAP], slot_win_ref[i * CAP + 1])
            for k in range(CAP):
                out_ref[i, k * LINES:(k + 1) * LINES] = slot_ref[i * CAP + k]
            out_ref[i, CAP * LINES:] = window.astype(F32).astype(BF16)
            return carry

        lax.fori_loop(0, tiles, pack, 0)


def resample(granule_blocks, row_weights, column_bank, destination, window_index, bank_index, tiles):
    blocks = granule_blocks.shape[0]
    deep = BANDS * SRC_ROWS
    lane = np.arange(256)
    depth = np.arange(WIN_ROWS * SRC_ROWS)
    spread = np.stack(
        [
            (depth[:, None] == r * SRC_ROWS + lane[None, :] % SRC_ROWS) & (lane[None, :] < deep)
            for r in range(WIN_ROWS)
        ]
    )
    mask = lane[None, :] // SRC_ROWS == np.arange(LINES)[:, None] // WIN_ROWS
    return pl.pallas_call(
        resample_kernel,
        grid_spec=pltpu.PrefetchScalarGridSpec(
            num_scalar_prefetch=3,
            grid=(blocks // STEP_BLOCKS,),
            in_specs=[
                pl.BlockSpec((WIN_ROWS * SRC_ROWS, blocks), lambda i, *_: (0, 0)),
                pl.BlockSpec((STEP_BLOCKS, deep, TILE_COLS), lambda i, *_: (i, 0, 0)),
                pl.BlockSpec(column_bank.shape, lambda i, *_: (0, 0, 0)),
                pl.BlockSpec(spread.shape, lambda i, *_: (0, 0, 0)),
                pl.BlockSpec(mask.shape, lambda i, *_: (0, 0)),
            ],
            out_specs=pl.BlockSpec((tiles, PACKED, TILE_COLS), lambda i, *_: (0, 0, 0)),
            scratch_shapes=[
                pltpu.VMEM((tiles * CAP, LINES, TILE_COLS), BF16),
                pltpu.SMEM((tiles * CAP,), jnp.int32),
                pltpu.SMEM((tiles,), jnp.int32),
                pltpu.VMEM((2, blocks * WIN_ROWS, 128), F32),
            ],
        ),
        out_shape=jax.ShapeDtypeStruct((tiles, PACKED, TILE_COLS), BF16),
        compiler_params=pltpu.CompilerParams(vmem_limit_bytes=VMEM_BYTES),
        name="resample",
    )(
        destination, window_index, bank_index,
        row_weights.transpose(1, 2, 0).reshape(WIN_ROWS * SRC_ROWS, blocks),
        granule_blocks.reshape(blocks, deep, TILE_COLS),
        column_bank, jnp.asarray(spread, BF16), jnp.asarray(mask, F32),
    )


def grid_kernel(
    got_ref, perm_ref, grid_ref, main_ref, left_ref, right_ref,
    sum_ref, number_ref, win_ref, count_ref, sem,
):
    tiles = got_ref.shape[0]
    numbers = got_ref[:, CAP * LINES:, :].astype(F32)
    number_ref[...] = jnp.max(numbers, axis=1).astype(jnp.int32)
    copy = pltpu.make_async_copy(number_ref, win_ref, sem)
    copy.start()

    def clear(w, carry):
        sum_ref[w] = jnp.zeros(sum_ref.shape[1:], F32)
        count_ref[w] = 0
        return carry

    lax.fori_loop(0, NWIN + 1, clear, 0)
    copy.wait()

    def add(t, carry):
        for k in range(CAP):
            w = win_ref[t, k]
            w = jnp.where(w < 0, NWIN, w)
            block = got_ref[t, k * LINES:(k + 1) * LINES].astype(F32)
            sum_ref[w, 0:LINES] = sum_ref[w, 0:LINES] + block
            count_ref[w] = count_ref[w] + 1
        return carry

    lax.fori_loop(0, tiles, add, 0, unroll=2)

    def finish(group, carry):
        first = group * GROUP
        means = []
        for k in range(GROUP):
            w = first + k
            divisor = jnp.maximum(count_ref[w], 1).astype(F32)
            mean = (sum_ref[w, 0:LINES] / divisor).astype(BF16).astype(F32)
            sum_ref[w, 0:LINES] = mean
            means.append(mean)
        row = pl.multiple_of(first * WIN_ROWS, GROUP * WIN_ROWS)
        for b in range(BANDS):
            part = jnp.concatenate([m[b * WIN_ROWS:(b + 1) * WIN_ROWS] for m in means], axis=0)
            grid_ref[b, pl.ds(row, GROUP * WIN_ROWS), :] = part.astype(BF16)
        for pair in range(GROUP // 2):
            lines = jnp.concatenate(
                [
                    sum_ref[first + pair * 2 + k, pl.ds(r, 16, stride=WIN_ROWS), :]
                    for k in range(2)
                    for r in range(WIN_ROWS)
                ],
                axis=0,
            )
            both = dot_nt(perm_ref[...], lines.astype(BF16)).astype(BF16)
            for k in range(2):
                w = first + pair * 2 + k
                turned = both[:, k * 128:(k + 1) * 128]
                main_ref[pl.ds(pl.multiple_of(w * 128, 128), 128), :] = turned[0:128]
                left_ref[pl.ds(pl.multiple_of(w * 16, 16), 16), :] = turned[128:144]
                right_ref[pl.ds(pl.multiple_of(w * 16, 16), 16), :] = turned[144:160]
        return carry

    lax.fori_loop(0, NWIN // GROUP, finish, 0)


def grid(received):
    tiles = received.shape[0]
    perm = np.zeros((TILE_COLS + 32, TILE_COLS), np.float32)
    for p in range(PHASES):
        for a in range(SPOTS):
            perm[p * SPOTS + a, a * PHASES + p] = 1.0
        for a in range(HALO):
            perm[128 + p * HALO + a, a * PHASES + p] = 1.0
            perm[144 + p * HALO + a, (SPOTS - HALO + a) * PHASES + p] = 1.0
    vmem = pl.BlockSpec(memory_space=pltpu.VMEM)
    return pl.pallas_call(
        grid_kernel,
        in_specs=[vmem, vmem],
        out_specs=[vmem] * 4,
        out_shape=[
            jax.ShapeDtypeStruct((BANDS, NWIN * WIN_ROWS, TILE_COLS), BF16),
            jax.ShapeDtypeStruct((NWIN * 128, 128), BF16),
            jax.ShapeDtypeStruct((NWIN * 16, 128), BF16),
            jax.ShapeDtypeStruct((NWIN * 16, 128), BF16),
        ],
        scratch_shapes=[
            pltpu.VMEM((NWIN + 1, 128, TILE_COLS), F32),
            pltpu.VMEM((tiles, TILE_COLS), jnp.int32),
            pltpu.SMEM((tiles, TILE_COLS), jnp.int32),
            pltpu.SMEM((NWIN + 1,), jnp.int32),
            pltpu.SemaphoreType.DMA,
        ],
        compiler_params=pltpu.CompilerParams(vmem_limit_bytes=VMEM_BYTES),
        name="grid",
    )(received, jnp.asarray(perm, BF16))


def exchange(main, left, right):
    across, down = lax.axis_size("tx"), lax.axis_size("ty")
    right_ward = [(i, i + 1) for i in range(across - 1)]
    left_ward = [(t, s) for s, t in right_ward]
    down_ward = [(i, i + 1) for i in range(down - 1)]
    up_ward = [(t, s) for s, t in down_ward]
    from_left = lax.ppermute(right, "tx", right_ward)
    from_right = lax.ppermute(left, "tx", left_ward)
    m, h = HALO * 128, HALO * 16
    first = jnp.concatenate([main[:m], from_left[:h], from_right[:h]], axis=0)
    last = jnp.concatenate([main[-m:], from_left[-h:], from_right[-h:]], axis=0)
    from_above = lax.ppermute(last, "ty", down_ward)
    from_below = lax.ppermute(first, "ty", up_ward)
    return from_left, from_right, from_above, from_below


def spread_matrix():
    out = np.zeros((PHASES + 2, GROUP_POINTS, GROUP * 48), np.float32)
    for index in range(PHASES + 2):
        p = (index - 1) % PHASES
        shift = -1 if index == 0 else (1 if index == PHASES + 1 else 0)
        for k in range(GROUP):
            for a in range(WIDE):
                s = a + shift
                row = k * WIDE + a
                if s < 0 or s >= WIDE:
                    continue
                if s < HALO:
                    out[index, row, GROUP * 16 + k * 16 + p * HALO + s] = 1.0
                elif s < HALO + SPOTS:
                    out[index, row, k * 16 + s - HALO] = 1.0
                else:
                    out[index, row, GROUP * 32 + k * 16 + p * HALO + s - HALO - SPOTS] = 1.0
    return out


def relu(x):
    return jnp.maximum(x, 0.0)


def encoder_kernel(
    main_ref, fl_ref, fr_ref, above_ref, below_ref, spread_ref, one_ref, down2_ref,
    two_ref, down3_hbm, three_hbm, down4_hbm, four_hbm,
    out_ref,
    ext1, ext2, x1, x2, d2, d3, d4, flat, down3_ref, three_ref, down4_ref, four_ref, sems,
):
    copies = [
        pltpu.make_async_copy(src, dst, sems.at[i])
        for i, (src, dst) in enumerate(
            (
                (down3_hbm, down3_ref),
                (three_hbm, three_ref),
                (down4_hbm, down4_ref),
                (four_hbm, four_ref),
            )
        )
    ]
    for copy in copies:
        copy.start()

    for h in range(HALO):
        for source, w in ((above_ref, h), (below_ref, HALO + NWIN + h)):
            ext1[w, 0:128] = source[h * 128:(h + 1) * 128]
            base = HALO * 128 + h * 16
            ext1[w, 128:144] = source[base:base + 16]
            ext1[w, 144:160] = source[base + HALO * 16:base + HALO * 16 + 16]

    def gather(w, carry):
        ext1[w + HALO, 0:128] = main_ref[pl.ds(pl.multiple_of(w * 128, 128), 128), :]
        ext1[w + HALO, 128:144] = fl_ref[pl.ds(pl.multiple_of(w * 16, 16), 16), :]
        ext1[w + HALO, 144:160] = fr_ref[pl.ds(pl.multiple_of(w * 16, 16), 16), :]
        return carry

    lax.fori_loop(0, NWIN, gather, 0)

    low = lax.broadcasted_iota(jnp.int32, (160, 128), 1) < 64

    def lower(w, carry):
        after = jnp.minimum(w + 1, TALL - 1)
        both = jnp.where(low, ext1[after].astype(F32), ext1[w].astype(F32))
        ext2[w] = pltpu.roll(both, 64, 1).astype(BF16)
        return carry

    lax.fori_loop(0, TALL, lower, 0)

    def place(g, carry):
        row = pl.multiple_of(g * GROUP_POINTS, GROUP_POINTS)
        for index in range(PHASES + 2):
            p = (index - 1) % PHASES
            sides = []
            for ext in (ext1, ext2):
                pieces = [ext[g * GROUP + k, p * 16:(p + 1) * 16] for k in range(GROUP)]
                pieces += [ext[g * GROUP + k, 128:144] for k in range(GROUP)]
                pieces += [ext[g * GROUP + k, 144:160] for k in range(GROUP)]
                sides.append(jnp.concatenate(pieces, axis=0))
            laid = dot(spread_ref[index], jnp.concatenate(sides, axis=1)).astype(BF16)
            x1[index, pl.ds(row, GROUP_POINTS), :] = laid[:, 0:128]
            x2[index, pl.ds(row, GROUP_POINTS), :] = laid[:, 128:256]
        return carry

    lax.fori_loop(0, TALL // GROUP, place, 0)

    across, below = lax.axis_size("tx"), lax.axis_size("ty")
    x, y = lax.axis_index("tx"), lax.axis_index("ty")
    least_w, most_w = jnp.where(y > 0, 0, HALO), jnp.where(y < below - 1, TALL, HALO + NWIN)
    least_a, most_a = jnp.where(x > 0, 0, HALO), jnp.where(x < across - 1, WIDE, HALO + SPOTS)
    point = lax.broadcasted_iota(jnp.int32, (POINTS, 128), 0)
    w = (point * (65536 // WIDE + 1)) >> 16
    a = point - w * WIDE
    inside = (w >= least_w) & (w < most_w) & (a >= least_a) & (a < most_a)
    mask = inside.astype(F32)
    mask2 = jnp.concatenate([mask, mask], axis=1)
    mask4 = jnp.concatenate([mask2, mask2], axis=1)

    def put(dst, i, j, value, last):
        rows = [(i + 1, 0)]
        if i == last:
            rows.append((0, WIDE))
        if i == 0:
            rows.append((last + 2, -WIDE))
        cols = [(j + 1, 0)]
        if j == last:
            cols.append((0, 1))
        if j == 0:
            cols.append((last + 2, -1))
        for r, row_shift in rows:
            for c, col_shift in cols:
                shift = (row_shift + col_shift) % POINTS
                moved = pltpu.roll(value, shift, 0) if shift else value
                dst[r, c] = moved.astype(BF16)

    for cb in range(4):
        for version, x in enumerate((x1, x2)):
            taps = jnp.concatenate([x[2 * cb + k] for k in range(4)], axis=1)
            level = relu(dot(taps, one_ref[...])).astype(BF16)
            for half in range(2):
                down = relu(dot(level[:, half * 256:(half + 1) * 256], down2_ref[...]))
                if version == 0:
                    rb = 1 + half
                elif half == 0:
                    rb = 3
                else:
                    rb = 0
                    down = pltpu.roll(down, WIDE, 0)
                put(d2, rb, cb, down * mask, 3)

    copies[0].wait()
    for rp in range(2):
        for j in range(2):
            total = None
            for v2 in range(2):
                taps = jnp.concatenate(
                    [d2[2 * rp + r, 2 * j + v2 + v] for r in range(4) for v in range(3)], axis=1
                )
                level = relu(dot(taps, two_ref[...])).astype(BF16)
                part = dot(level, down3_ref[v2])
                total = part if total is None else total + part
            put(d3, rp, j, relu(total) * mask2, 1)

    copies[1].wait()
    copies[2].wait()
    total = None
    for i in range(2):
        for j in range(2):
            taps = jnp.concatenate(
                [d3[i + u, j + v] for u in range(3) for v in range(3)], axis=1
            )
            level = relu(dot(taps, three_ref[...])).astype(BF16)
            part = dot(level, down4_ref[i * 2 + j])
            total = part if total is None else total + part
    put(d4, 0, 0, relu(total) * mask4, 0)

    copies[3].wait()
    first, count = HALO * WIDE, NWIN * WIDE
    taps = jnp.concatenate(
        [d4[u, v, first:first + count] for u in range(3) for v in range(3)], axis=1
    )
    flat[...] = relu(dot(taps, four_ref[...]))
    for w in range(NWIN):
        start = w * WIDE + HALO
        out_ref[w] = flat[start:start + SPOTS].astype(BF16)


def encoder(main, halos, one, down2, two, down3, three, down4, four):
    vmem = pl.BlockSpec(memory_space=pltpu.VMEM)
    hbm = pl.BlockSpec(memory_space=pl.ANY)
    return pl.pallas_call(
        encoder_kernel,
        in_specs=[vmem] * 9 + [hbm] * 4,
        out_specs=vmem,
        out_shape=jax.ShapeDtypeStruct((NWIN, SPOTS, four.shape[-1]), BF16),
        scratch_shapes=[
            pltpu.VMEM((TALL, 160, 128), BF16),
            pltpu.VMEM((TALL, 160, 128), BF16),
            pltpu.VMEM((PHASES + 2, POINTS, 128), BF16),
            pltpu.VMEM((PHASES + 2, POINTS, 128), BF16),
            pltpu.VMEM((6, 6, POINTS, 128), BF16),
            pltpu.VMEM((4, 4, POINTS, 256), BF16),
            pltpu.VMEM((3, 3, POINTS, 512), BF16),
            pltpu.VMEM((NWIN * WIDE, 512), F32),
            pltpu.VMEM(down3.shape, BF16),
            pltpu.VMEM(three.shape, BF16),
            pltpu.VMEM(down4.shape, BF16),
            pltpu.VMEM(four.shape, BF16),
            pltpu.SemaphoreType.DMA((4,)),
        ],
        compiler_params=pltpu.CompilerParams(vmem_limit_bytes=VMEM_BYTES),
        name="encoder",
    )(
        main, *halos, jnp.asarray(spread_matrix(), BF16), one, down2,
        two, down3, three, down4, four,
    )


def level_one_weights(kernel):
    kernel = jnp.pad(kernel, ((0, 0), (0, 0), (0, 16 - BANDS), (0, 0)))
    columns = []
    for rb in range(2):
        for i in range(2):
            for j in range(2):
                top = 1 + 2 * rb + i
                wide = jnp.pad(kernel, ((top, 5 - top), (j, 1 - j), (0, 0), (0, 0)))
                columns.append(wide.transpose(1, 0, 2, 3).reshape(4 * 8 * 16, -1))
    return jnp.concatenate(columns, axis=1)


def level_two_weights(kernel):
    none = ((0, 0),) * 3
    pair = [jnp.pad(kernel, ((i, 1 - i),) + none) for i in range(2)]
    return jnp.concatenate(pair, axis=3).reshape(12 * kernel.shape[2], -1)


def body(
    granule_blocks, row_weights, column_bank, destination, window_index, bank_index,
    kernel_one, reduce_two, kernel_two, reduce_three, kernel_three, reduce_four, kernel_four,
):
    axes = ("tx", "ty")
    tiles = lax.axis_size("tx") * lax.axis_size("ty")
    slots = resample(
        granule_blocks, row_weights, column_bank, destination, window_index, bank_index, tiles
    )
    received = lax.all_to_all(slots, axes, split_axis=0, concat_axis=0, tiled=True)
    gridded, main, left, right = grid(received)
    halos = exchange(main, left, right)
    flat = encoder(
        main, halos,
        level_one_weights(kernel_one),
        reduce_two.reshape(256, 128),
        level_two_weights(kernel_two),
        reduce_three.transpose(1, 0, 2, 3).reshape(2, 256, 256),
        kernel_three.reshape(9 * 256, 256),
        reduce_four.reshape(4, 256, 512),
        kernel_four.reshape(9 * 512, 512),
    )
    return gridded, flat.transpose(2, 0, 1)


def solution(mesh):
    both = P(("tx", "ty"))
    in_specs = (both, both, P(), both, both, both) + (P(),) * 7
    out_specs = (P(None, "ty", "tx"), P(None, "ty", "tx"))
    return jax.shard_map(body, mesh=mesh, in_specs=in_specs, out_specs=out_specs, check_vma=False)
```

profile of v0, /device:TPU:1, one launch (start us, length us, event | category | flops | bytes accessed | tf_op | source)
XLA Modules:
  0.0 113.8 jit_solution(14618139425122462190)
XLA Ops:
  0.6 9.0 %resample.1 = bf16[32,216,128]{2,1,0:T(8,128)(2,1)} custom-call(s32[64]{0:T(128)} %dest_ref.1, s32[64]{0:T(128)} %win_ref.1, s32[64]{0:T(128)} %choice_ref.1, bf16[128,64]{1,0:T(8,128)(2,1)} %bitcast.53, bf16[64,208,128]{2,1,0:T(8,128)(2,1)} %bitcast.37, bf16[8,128,128]{2,1,0:T(8,128)(2,1)} %bank_ref.1, bf16[8,128,256]{2,1,0:T(8,128)(2,1)} %constant.11.clone.spread_ref, ...), custom_call_target="tpu_custom_call" | custom-call | tf_op jit(solution)/shard_map/resample/pallas_call | solution.py:107
  9.7 7.1 %all-to-all-start = ((bf16[32,216,128]{2,1,0:T(8,128)(2,1)}), bf16[32,216,128]{2,1,0:T(8,128)(2,1)S(1)}, u32[]{:S(2)}, u32[]{:S(2)}) async-start(bf16[32,216,128]{2,1,0:T(8,128)(2,1)} %resample.1), calls=%async_computation | async-start | bytes 3538944 | tf_op jit(solution)/shard_map/all_to_all | solution.py:474
  16.8 0.0 copy-done.7
  16.8 0.0 copy-start.2
  16.8 0.2 pad_bitcast_fusion
  17.2 0.6 copy-done.2
  17.8 0.7 copy.27
  18.5 1.2 %concatenate.14.one_ref = bf16[512,512]{1,0:T(8,128)(2,1)} concatenate(bf16[512,64]{1,0:T(8,128)(2,1)S(1)} %bitcast.42, bf16[512,64]{1,0:T(8,128)(2,1)S(1)} %bitcast.43, bf16[512,64]{1,0:T(8,128)(2,1)S(1)} %bitcast.44, bf16[512,64]{1,0:T(8,128)(2,1)S(1)} %bitcast.45, bf16[512,64]{1,0:T(8,128)(2,1)S(1)} %bitcast.46, bf16[512,64]{1,0:T(8,128)(2,1)S(1)} %bitcast.47, ...), dimensions={1} | concatenate | bytes 1048576 | tf_op jit(solution)/shard_map/concatenate | solution.py:456
  19.6 39.6 %all-to-all-done.got_ref = bf16[32,216,128]{2,1,0:T(8,128)(2,1)S(1)} async-done(((bf16[32,216,128]{2,1,0:T(8,128)(2,1)}), bf16[32,216,128]{2,1,0:T(8,128)(2,1)S(1)}, u32[]{:S(2)}, u32[]{:S(2)}) %all-to-all-start) | async-done | bytes 1769504 | tf_op jit(solution)/shard_map/all_to_all | solution.py:474
  59.2 1.3 %copy-done = bf16[32,216,128]{2,1,0:T(8,128)(2,1)} copy-done((bf16[32,216,128]{2,1,0:T(8,128)(2,1)}, bf16[32,216,128]{2,1,0:T(8,128)(2,1)S(1)}, u32[]{:S(2)}) %copy-start) | copy-done | bytes 1769496
  60.5 6.2 %grid.1 = (bf16[13,256,128]{2,1,0:T(8,128)(2,1)}, bf16[4096,128]{1,0:T(8,128)(2,1)}, bf16[512,128]{1,0:T(8,128)(2,1)}, bf16[512,128]{1,0:T(8,128)(2,1)}) custom-call(bf16[32,216,128]{2,1,0:T(8,128)(2,1)} %copy-done, bf16[160,128]{1,0:T(8,128)(2,1)} %constant.13.clone.perm_ref), custom_call_target="tpu_custom_call" | custom-call | tf_op jit(solution)/shard_map/grid/pallas_call | solution.py:211
  66.7 2.9 %collective-permute-start = (bf16[512,128]{1,0:T(8,128)(2,1)}, bf16[512,128]{1,0:T(8,128)(2,1)S(1)}, u32[]{:S(2)}, u32[]{:S(2)}) collective-permute-start(bf16[512,128]{1,0:T(8,128)(2,1)} %get-tuple-element.8), channel_id=1, source_target_pairs={{0,8},{8,16},{16,24},{1,9},{9,17},{17,25},{2,10},{10,18},{18,26},{... | collective-permute-start | bytes 393224 | tf_op jit(solution)/shard_map/ppermute | solution.py:239
  69.6 1.9 %collective-permute-start.1 = (bf16[512,128]{1,0:T(8,128)(2,1)}, bf16[512,128]{1,0:T(8,128)(2,1)S(1)}, u32[]{:S(2)}, u32[]{:S(2)}) collective-permute-start(bf16[512,128]{1,0:T(8,128)(2,1)} %get-tuple-element.9), channel_id=1, source_target_pairs={{8,0},{16,8},{24,16},{9,1},{17,9},{25,17},{10,2},{18,10},{26,18},{... | collective-permute-start | bytes 393224 | tf_op jit(solution)/shard_map/ppermute | solution.py:240
  71.5 0.9 fusion.3
  72.4 3.7 %collective-permute-done.1.fr_ref = bf16[512,128]{1,0:T(8,128)(2,1)S(1)} collective-permute-done((bf16[512,128]{1,0:T(8,128)(2,1)}, bf16[512,128]{1,0:T(8,128)(2,1)S(1)}, u32[]{:S(2)}, u32[]{:S(2)}) %collective-permute-start.1) | collective-permute-done | bytes 131104 | tf_op jit(solution)/shard_map/ppermute | solution.py:240
  76.1 0.0 collective-permute-done.fl_ref
  76.1 2.2 %collective-permute-start.2 = (bf16[320,128]{1,0:T(8,128)(2,1)S(1)}, bf16[320,128]{1,0:T(8,128)(2,1)S(1)}, u32[]{:S(2)}, u32[]{:S(2)}) collective-permute-start(bf16[320,128]{1,0:T(8,128)(2,1)S(1)} %pad_maximum_fusion), channel_id=1, source_target_pairs={{0,1},{1,2},{2,3},{3,4},{4,5},{5,6},{6,7},{8,9},{9,10},{10,11},{11... | collective-permute-start | bytes 245768 | tf_op jit(solution)/shard_map/ppermute | solution.py:244
  78.3 1.3 %collective-permute-start.3 = (bf16[320,128]{1,0:T(8,128)(2,1)S(1)}, bf16[320,128]{1,0:T(8,128)(2,1)S(1)}, u32[]{:S(2)}, u32[]{:S(2)}) collective-permute-start(bf16[320,128]{1,0:T(8,128)(2,1)S(1)} %pad_maximum_fusion.1), channel_id=1, source_target_pairs={{1,0},{2,1},{3,2},{4,3},{5,4},{6,5},{7,6},{9,8},{10,9},{11,10},{12... | collective-permute-start | bytes 245768 | tf_op jit(solution)/shard_map/ppermute | solution.py:245
  79.6 1.0 fusion.2
  80.6 0.0 collective-permute-done.2.above_ref
  80.6 2.9 %collective-permute-done.3.below_ref = bf16[320,128]{1,0:T(8,128)(2,1)S(1)} collective-permute-done((bf16[320,128]{1,0:T(8,128)(2,1)S(1)}, bf16[320,128]{1,0:T(8,128)(2,1)S(1)}, u32[]{:S(2)}, u32[]{:S(2)}) %collective-permute-start.3) | collective-permute-done | bytes 81952 | tf_op jit(solution)/shard_map/ppermute | solution.py:245
  83.5 0.0 copy-done.4
  83.5 0.6 copy-done.6
  84.1 29.5 %encoder.1 = bf16[32,16,512]{2,1,0:T(8,128)(2,1)} custom-call(bf16[4096,128]{1,0:T(8,128)(2,1)} %get-tuple-element.7.main_ref, bf16[512,128]{1,0:T(8,128)(2,1)} %copy-done.3, bf16[512,128]{1,0:T(8,128)(2,1)} %copy-done.4, bf16[320,128]{1,0:T(8,128)(2,1)} %copy-done.5, bf16[320,128]{1,0:T(8,128)(2,1)} %copy-done.6, ...), custom_call_target="tpu_custom_call" | custom-call | tf_op jit(solution)/shard_map/encoder/pallas_call | solution.py:419
  (23 shorter events, 0.1 us)
Async XLA Ops:
  9.7 7.1 %copy-start.7 = (bf16[3,3,13,64]{3,2,1,0:T(8,128)(2,1)S(1)}, bf16[3,3,13,64]{3,2,1,0:T(8,128)(2,1)}, u32[]{:S(2)}) copy-start(bf16[3,3,13,64]{3,2,1,0:T(8,128)(2,1)} %param.23) | copy-start | bytes 44932
  9.7 49.6 %all-to-all-start = ((bf16[32,216,128]{2,1,0:T(8,128)(2,1)}), bf16[32,216,128]{2,1,0:T(8,128)(2,1)S(1)}, u32[]{:S(2)}, u32[]{:S(2)}) async-start(bf16[32,216,128]{2,1,0:T(8,128)(2,1)} %resample.1), calls=%async_computation | async-start | bytes 3538944 | tf_op jit(solution)/shard_map/all_to_all | solution.py:474
  16.8 1.0 copy-start.2
  19.6 60.0 %copy-start.1 = (bf16[3,3,128,128]{3,2,1,0:T(8,128)(2,1)S(1)}, bf16[3,3,128,128]{3,2,1,0:T(8,128)(2,1)}, u32[]{:S(2)}) copy-start(bf16[3,3,128,128]{3,2,1,0:T(8,128)(2,1)} %param.25) | copy-start | bytes 884740
  59.2 1.3 %copy-start = (bf16[32,216,128]{2,1,0:T(8,128)(2,1)}, bf16[32,216,128]{2,1,0:T(8,128)(2,1)S(1)}, u32[]{:S(2)}) copy-start(bf16[32,216,128]{2,1,0:T(8,128)(2,1)S(1)} %all-to-all-done.got_ref) | copy-start | bytes 5308420
  66.7 9.4 %collective-permute-start = (bf16[512,128]{1,0:T(8,128)(2,1)}, bf16[512,128]{1,0:T(8,128)(2,1)S(1)}, u32[]{:S(2)}, u32[]{:S(2)}) collective-permute-start(bf16[512,128]{1,0:T(8,128)(2,1)} %get-tuple-element.8), channel_id=1, source_target_pairs={{0,8},{8,16},{16,24},{1,9},{9,17},{17,25},{2,10},{10,18},{18,26},{... | collective-permute-start | bytes 393224 | tf_op jit(solution)/shard_map/ppermute | solution.py:239
  69.6 6.5 %collective-permute-start.1 = (bf16[512,128]{1,0:T(8,128)(2,1)}, bf16[512,128]{1,0:T(8,128)(2,1)S(1)}, u32[]{:S(2)}, u32[]{:S(2)}) collective-permute-start(bf16[512,128]{1,0:T(8,128)(2,1)} %get-tuple-element.9), channel_id=1, source_target_pairs={{8,0},{16,8},{24,16},{9,1},{17,9},{25,17},{10,2},{18,10},{26,18},{... | collective-permute-start | bytes 393224 | tf_op jit(solution)/shard_map/ppermute | solution.py:240
  76.1 7.4 %copy-start.4 = (bf16[512,128]{1,0:T(8,128)(2,1)}, bf16[512,128]{1,0:T(8,128)(2,1)S(1)}, u32[]{:S(2)}) copy-start(bf16[512,128]{1,0:T(8,128)(2,1)S(1)} %collective-permute-done.1.fr_ref) | copy-start | bytes 393220
  76.1 7.4 %copy-start.3 = (bf16[512,128]{1,0:T(8,128)(2,1)}, bf16[512,128]{1,0:T(8,128)(2,1)S(1)}, u32[]{:S(2)}) copy-start(bf16[512,128]{1,0:T(8,128)(2,1)S(1)} %collective-permute-done.fl_ref) | copy-start | bytes 393220
  76.1 4.5 %collective-permute-start.2 = (bf16[320,128]{1,0:T(8,128)(2,1)S(1)}, bf16[320,128]{1,0:T(8,128)(2,1)S(1)}, u32[]{:S(2)}, u32[]{:S(2)}) collective-permute-start(bf16[320,128]{1,0:T(8,128)(2,1)S(1)} %pad_maximum_fusion), channel_id=1, source_target_pairs={{0,1},{1,2},{2,3},{3,4},{4,5},{5,6},{6,7},{8,9},{9,10},{10,11},{11... | collective-permute-start | bytes 245768 | tf_op jit(solution)/shard_map/ppermute | solution.py:244
  78.3 5.2 %collective-permute-start.3 = (bf16[320,128]{1,0:T(8,128)(2,1)S(1)}, bf16[320,128]{1,0:T(8,128)(2,1)S(1)}, u32[]{:S(2)}, u32[]{:S(2)}) collective-permute-start(bf16[320,128]{1,0:T(8,128)(2,1)S(1)} %pad_maximum_fusion.1), channel_id=1, source_target_pairs={{1,0},{2,1},{3,2},{4,3},{5,4},{6,5},{7,6},{9,8},{10,9},{11,10},{12... | collective-permute-start | bytes 245768 | tf_op jit(solution)/shard_map/ppermute | solution.py:245
  80.6 2.9 %copy-start.5 = (bf16[320,128]{1,0:T(8,128)(2,1)}, bf16[320,128]{1,0:T(8,128)(2,1)S(1)}, u32[]{:S(2)}) copy-start(bf16[320,128]{1,0:T(8,128)(2,1)S(1)} %collective-permute-done.2.above_ref) | copy-start | bytes 245764
  83.5 0.6 copy-start.6
where the time goes:
time: 114 us
  waiting for transfers between devices  46.2 us (41%)
  Pallas kernels  44.7 us (39%)
  starting transfers between devices  15.4 us (14%)
  local copies, waits for them, and re-layouts  5.56 us (5%)
    all_to_all x1, waiting for transfers between devices, body(): lax.all_to_all(slots, axes, split_axis=0, concat_axis=0, tiled=True)  39.6 us
    pallas_call x1, Pallas kernels, encoder(): pl.pallas_call(encoder_kernel, in_specs=[vmem] * 9 + [hbm] * 4, out_specs...  29.5 us
    pallas_call x1, Pallas kernels, resample(): pl.pallas_call(resample_kernel, grid_spec=pltpu.PrefetchScalarGridSpec(nu...  9.03 us
    all_to_all x1, starting transfers between devices, body(): lax.all_to_all(slots, axes, split_axis=0, concat_axis=0, tiled=True)  7.1 us
    pallas_call x1, Pallas kernels, grid(): pl.pallas_call(grid_kernel, in_specs=[vmem, vmem], out_specs=[vmem] * 4,...  6.18 us
    ppermute x1, waiting for transfers between devices, exchange(): from_right = lax.ppermute(left, 'tx', left_ward)  3.68 us
    ppermute x1, waiting for transfers between devices, exchange(): from_below = lax.ppermute(first, 'ty', up_ward)  2.91 us
    ppermute x1, starting transfers between devices, exchange(): from_left = lax.ppermute(right, 'tx', right_ward)  2.89 us
  transfers between devices with their start and end apart: 5, of which 3 were waited for; matrix products, arithmetic and copies ran while one was open for 4% of the time, Pallas kernels for 0%

commit v1 on v0

--- a/solution.py
+++ b/solution.py
@@ -17,8 +17,7 @@
 NWIN = 32
 TILE_COLS = 128
 LINES = BANDS * WIN_ROWS
-PACKED = CAP * LINES + WIN_ROWS
-STEP_BLOCKS = 8
+STEP_BLOCKS = 16
 PHASES = 8
 SPOTS = TILE_COLS // PHASES
 HALO = 2
@@ -39,108 +38,119 @@
 
 
 def resample_kernel(
-    dest_ref, win_ref, choice_ref, weight_ref, raw_ref, bank_ref, spread_ref, mask_ref,
-    out_ref, slot_ref, slot_win_ref, held_ref, rows_ref,
+    chosen, dest_ref, win_ref, choice_ref, weight_ref, raw_hbm, bank_ref, out_ref,
+    raw_ref, rows_ref, held_ref, block_ref, slot_win_ref, sems,
 ):
-    step = pl.program_id(0)
-    tiles = held_ref.shape[0]
-
-    @pl.when(step == 0)
-    def _():
-        def clear(i, carry):
-            held_ref[i] = 0
-            for k in range(CAP):
-                slot_win_ref[i * CAP + k] = -1
-            return carry
-
-        lax.fori_loop(0, tiles, clear, 0)
-        turned = jnp.transpose(weight_ref[...].astype(F32)).astype(BF16)
-        blocks = turned.shape[0]
-        for r in range(WIN_ROWS):
-            wide = dot(turned, spread_ref[r])
-            for h in range(2):
-                rows_ref[h, pl.ds(r, blocks, stride=WIN_ROWS), :] = wide[:, h * 128:(h + 1) * 128]
-
-    mask = mask_ref[...]
-    rowed = []
-    for j in range(STEP_BLOCKS):
-        row = pl.multiple_of((step * STEP_BLOCKS + j) * WIN_ROWS, WIN_ROWS)
-        rows = jnp.concatenate([rows_ref[h, pl.ds(row, WIN_ROWS), :] for h in range(2)], axis=1)
-        weights = jnp.concatenate([rows] * BANDS, axis=0) * mask
-        weights = weights.astype(BF16)[:, 0:BANDS * SRC_ROWS]
-        rowed.append(dot(weights, raw_ref[j]).astype(BF16))
-    for j in range(STEP_BLOCKS):
-        n = step * STEP_BLOCKS + j
+    tiles, blocks = held_ref.shape[0], dest_ref.shape[0]
+    deep = BANDS * SRC_ROWS
+
+    def clear(i, carry):
+        held_ref[i] = 0
+        block_ref[i] = 0
+        for k in range(CAP):
+            slot_win_ref[i * CAP + k] = -1
+        return carry
+
+    lax.fori_loop(0, tiles, clear, 0, unroll=4)
+
+    def find(n, carry):
         tile = dest_ref[n]
         rank = held_ref[tile]
         held_ref[tile] = rank + 1
-        slot = tile * CAP + rank
-        slot_win_ref[slot] = win_ref[n]
-        slot_ref[slot] = dot(rowed[j], bank_ref[choice_ref[n]]).astype(BF16)
-
-    @pl.when(step == pl.num_programs(0) - 1)
-    def _():
-        lane = lax.broadcasted_iota(jnp.int32, (WIN_ROWS, TILE_COLS), 1)
-
-        def pack(i, carry):
-            window = jnp.where(lane == 0, slot_win_ref[i * CAP], slot_win_ref[i * CAP + 1])
-            for k in range(CAP):
-                out_ref[i, k * LINES:(k + 1) * LINES] = slot_ref[i * CAP + k]
-            out_ref[i, CAP * LINES:] = window.astype(F32).astype(BF16)
-            return carry
-
-        lax.fori_loop(0, tiles, pack, 0)
-
-
-def resample(granule_blocks, row_weights, column_bank, destination, window_index, bank_index, tiles):
+        slot_win_ref[tile * CAP + rank] = win_ref[n]
+        block_ref[tile] = jnp.where(rank == chosen, n, block_ref[tile])
+        return carry
+
+    lax.fori_loop(0, blocks, find, 0, unroll=4)
+
+    def fetch(t):
+        return pltpu.make_async_copy(raw_hbm.at[block_ref[t]], raw_ref.at[t], sems.at[t])
+
+    def start(t, carry):
+        fetch(t).start()
+        return carry
+
+    lax.fori_loop(0, tiles, start, 0)
+
+    turned = jnp.transpose(weight_ref[...].astype(F32)).astype(BF16)
+    depth = lax.broadcasted_iota(jnp.int32, (WIN_ROWS * SRC_ROWS, 256), 0)
+    lane = lax.broadcasted_iota(jnp.int32, (WIN_ROWS * SRC_ROWS, 256), 1)
+    offset = depth - (lane & (SRC_ROWS - 1))
+    for r in range(WIN_ROWS):
+        wide = dot(turned, (offset == r * SRC_ROWS).astype(F32).astype(BF16))
+        for h in range(2):
+            rows_ref[h, pl.ds(r, blocks, stride=WIN_ROWS), :] = wide[:, h * 128:(h + 1) * 128]
+
+    line = lax.broadcasted_iota(jnp.int32, (LINES, 256), 0)
+    lane = lax.broadcasted_iota(jnp.int32, (LINES, 256), 1)
+    own = (line >> 3) == (lane >> 4)
+    spot = lax.broadcasted_iota(jnp.int32, (WIN_ROWS, TILE_COLS), 1)
+
+    def work(group, carry):
+        rowed = []
+        for j in range(STEP_BLOCKS):
+            t = group * STEP_BLOCKS + j
+            fetch(t).wait()
+            row = pl.multiple_of(block_ref[t] * WIN_ROWS, WIN_ROWS)
+            rows = jnp.concatenate(
+                [rows_ref[h, pl.ds(row, WIN_ROWS), :] for h in range(2)], axis=1
+            )
+            weights = jnp.where(own, jnp.concatenate([rows] * BANDS, axis=0), 0.0)
+            rowed.append(dot(weights.astype(BF16)[:, 0:deep], raw_ref[t]).astype(BF16))
+        for j in range(STEP_BLOCKS):
+            t = group * STEP_BLOCKS + j
+            bank = bank_ref[choice_ref[block_ref[t]]]
+            out_ref[t, 0:LINES] = dot(rowed[j], bank).astype(BF16)
+            if chosen == 0:
+                window = jnp.where(spot == 0, slot_win_ref[t * CAP], slot_win_ref[t * CAP + 1])
+                out_ref[t, LINES:] = window.astype(F32).astype(BF16)
+        return carry
+
+    lax.fori_loop(0, tiles // STEP_BLOCKS, work, 0)
+
+
+def resample(
+    chosen, granule_blocks, row_weights, column_bank, destination, window_index, bank_index, tiles
+):
     blocks = granule_blocks.shape[0]
     deep = BANDS * SRC_ROWS
-    lane = np.arange(256)
-    depth = np.arange(WIN_ROWS * SRC_ROWS)
-    spread = np.stack(
-        [
-            (depth[:, None] == r * SRC_ROWS + lane[None, :] % SRC_ROWS) & (lane[None, :] < deep)
-            for r in range(WIN_ROWS)
-        ]
-    )
-    mask = lane[None, :] // SRC_ROWS == np.arange(LINES)[:, None] // WIN_ROWS
+    height = LINES + (WIN_ROWS if chosen == 0 else 0)
+    vmem = pl.BlockSpec(memory_space=pltpu.VMEM)
+    smem = pl.BlockSpec(memory_space=pltpu.SMEM)
     return pl.pallas_call(
-        resample_kernel,
-        grid_spec=pltpu.PrefetchScalarGridSpec(
-            num_scalar_prefetch=3,
-            grid=(blocks // STEP_BLOCKS,),
-            in_specs=[
-                pl.BlockSpec((WIN_ROWS * SRC_ROWS, blocks), lambda i, *_: (0, 0)),
-                pl.BlockSpec((STEP_BLOCKS, deep, TILE_COLS), lambda i, *_: (i, 0, 0)),
-                pl.BlockSpec(column_bank.shape, lambda i, *_: (0, 0, 0)),
-                pl.BlockSpec(spread.shape, lambda i, *_: (0, 0, 0)),
-                pl.BlockSpec(mask.shape, lambda i, *_: (0, 0)),
-            ],
-            out_specs=pl.BlockSpec((tiles, PACKED, TILE_COLS), lambda i, *_: (0, 0, 0)),
-            scratch_shapes=[
-                pltpu.VMEM((tiles * CAP, LINES, TILE_COLS), BF16),
-                pltpu.SMEM((tiles * CAP,), jnp.int32),
-                pltpu.SMEM((tiles,), jnp.int32),
-                pltpu.VMEM((2, blocks * WIN_ROWS, 128), F32),
-            ],
+        functools.partial(resample_kernel, chosen),
+        in_specs=[smem, smem, smem, vmem, pl.BlockSpec(memory_space=pl.ANY), vmem],
+        out_specs=vmem,
+        scratch_shapes=[
+            pltpu.VMEM((tiles, deep, TILE_COLS), BF16),
+            pltpu.VMEM((2, blocks * WIN_ROWS, 128), F32),
+            pltpu.SMEM((tiles,), jnp.int32),
+            pltpu.SMEM((tiles,), jnp.int32),
+            pltpu.SMEM((tiles * CAP,), jnp.int32),
+            pltpu.SemaphoreType.DMA((tiles,)),
+        ],
+        out_shape=jax.ShapeDtypeStruct((tiles, height, TILE_COLS), BF16),
+        compiler_params=pltpu.CompilerParams(vmem_limit_bytes=VMEM_BYTES),
+        cost_estimate=pl.CostEstimate(
+            flops=2 * tiles * LINES * 128 * 384,
+            bytes_accessed=tiles * 80000 * 8,
+            transcendentals=0,
         ),
-        out_shape=jax.ShapeDtypeStruct((tiles, PACKED, TILE_COLS), BF16),
-        compiler_params=pltpu.CompilerParams(vmem_limit_bytes=VMEM_BYTES),
-        name="resample",
+        name=f"resample_{chosen}",
     )(
         destination, window_index, bank_index,
         row_weights.transpose(1, 2, 0).reshape(WIN_ROWS * SRC_ROWS, blocks),
         granule_blocks.reshape(blocks, deep, TILE_COLS),
-        column_bank, jnp.asarray(spread, BF16), jnp.asarray(mask, F32),
+        column_bank,
     )
 
 
 def grid_kernel(
-    got_ref, perm_ref, grid_ref, main_ref, left_ref, right_ref,
+    got0_ref, got1_ref, perm_ref, grid_ref, main_ref, left_ref, right_ref,
     sum_ref, number_ref, win_ref, count_ref, sem,
 ):
-    tiles = got_ref.shape[0]
-    numbers = got_ref[:, CAP * LINES:, :].astype(F32)
+    tiles = got0_ref.shape[0]
+    numbers = got0_ref[:, LINES:, :].astype(F32)
     number_ref[...] = jnp.max(numbers, axis=1).astype(jnp.int32)
     copy = pltpu.make_async_copy(number_ref, win_ref, sem)
     copy.start()
@@ -154,10 +164,10 @@
     copy.wait()
 
     def add(t, carry):
-        for k in range(CAP):
+        for k, got_ref in enumerate((got0_ref, got1_ref)):
             w = win_ref[t, k]
             w = jnp.where(w < 0, NWIN, w)
-            block = got_ref[t, k * LINES:(k + 1) * LINES].astype(F32)
+            block = got_ref[t, 0:LINES].astype(F32)
             sum_ref[w, 0:LINES] = sum_ref[w, 0:LINES] + block
             count_ref[w] = count_ref[w] + 1
         return carry
@@ -198,8 +208,8 @@
     lax.fori_loop(0, NWIN // GROUP, finish, 0)
 
 
-def grid(received):
-    tiles = received.shape[0]
+def grid(first, second):
+    tiles = first.shape[0]
     perm = np.zeros((TILE_COLS + 32, TILE_COLS), np.float32)
     for p in range(PHASES):
         for a in range(SPOTS):
@@ -210,7 +220,7 @@
     vmem = pl.BlockSpec(memory_space=pltpu.VMEM)
     return pl.pallas_call(
         grid_kernel,
-        in_specs=[vmem, vmem],
+        in_specs=[vmem] * 3,
         out_specs=[vmem] * 4,
         out_shape=[
             jax.ShapeDtypeStruct((BANDS, NWIN * WIN_ROWS, TILE_COLS), BF16),
@@ -227,7 +237,7 @@
         ],
         compiler_params=pltpu.CompilerParams(vmem_limit_bytes=VMEM_BYTES),
         name="grid",
-    )(received, jnp.asarray(perm, BF16))
+    )(first, second, jnp.asarray(perm, BF16))
 
 
 def exchange(main, left, right):
@@ -468,11 +478,17 @@
 ):
     axes = ("tx", "ty")
     tiles = lax.axis_size("tx") * lax.axis_size("ty")
-    slots = resample(
-        granule_blocks, row_weights, column_bank, destination, window_index, bank_index, tiles
-    )
-    received = lax.all_to_all(slots, axes, split_axis=0, concat_axis=0, tiled=True)
-    gridded, main, left, right = grid(received)
+    received = [
+        lax.all_to_all(
+            resample(
+                chosen, granule_blocks, row_weights, column_bank, destination, window_index,
+                bank_index, tiles,
+            ),
+            axes, split_axis=0, concat_axis=0, tiled=True,
+        )
+        for chosen in range(CAP)
+    ]
+    gridded, main, left, right = grid(*received)
     halos = exchange(main, left, right)
     flat = encoder(
         main, halos,

time: 114 us -> 122 us (1.070)
  Pallas kernels: 44.7 us -> 54.5 us
  waiting for transfers between devices: 46.2 us -> 41.4 us
  starting transfers between devices: 15.4 us -> 18.6 us
    pallas_call x2 -> x3, Pallas kernels: 15.2 us -> 25 us  [the longest x2 18.8 us: resample(): pl.pallas_call(functools.partial(resample_kernel, chosen), in_specs=[smem...]
    all_to_all x1 -> x2, waiting for transfers between devices: 39.6 us -> 34.8 us  [body(): lax.all_to_all(resample(chosen, granule_blocks, row_weights, column_bank,...]
    all_to_all x1 -> x2, starting transfers between devices: 7.1 us -> 10.2 us  [body(): lax.all_to_all(resample(chosen, granule_blocks, row_weights, column_bank,...]
    unnamed x16 -> x18, local copies, waits for them, and re-layouts: 2.47 us -> 2.13 us
  transfers between devices with their start and end apart: 5 -> 6, of which waited for: 3 -> 4; matrix products, arithmetic and copies ran while one was open for 4% -> 3% of each run, Pallas kernels for 0% -> 8%
where the time goes in v1:
time: 122 us
  Pallas kernels  54.5 us (45%)
  waiting for transfers between devices  41.4 us (34%)
  starting transfers between devices  18.6 us (15%)
  local copies, waits for them, and re-layouts  5.22 us (4%)
    all_to_all x2, waiting for transfers between devices, body(): lax.all_to_all(resample(chosen, granule_blocks, row_weights, column_bank,...  34.8 us
    pallas_call x1, Pallas kernels, encoder(): pl.pallas_call(encoder_kernel, in_specs=[vmem] * 9 + [hbm] * 4, out_specs...  29.5 us
    pallas_call x2, Pallas kernels, resample(): pl.pallas_call(functools.partial(resample_kernel, chosen), in_specs=[smem...  18.8 us
    all_to_all x2, starting transfers between devices, body(): lax.all_to_all(resample(chosen, granule_blocks, row_weights, column_bank,...  10.2 us
    pallas_call x1, Pallas kernels, grid(): pl.pallas_call(grid_kernel, in_specs=[vmem] * 3, out_specs=[vmem] * 4, ou...  6.13 us
    ppermute x1, waiting for transfers between devices, exchange(): from_right = lax.ppermute(left, 'tx', left_ward)  3.68 us
    ppermute x1, starting transfers between devices, exchange(): from_left = lax.ppermute(right, 'tx', right_ward)  2.89 us
    ppermute x1, waiting for transfers between devices, exchange(): from_below = lax.ppermute(first, 'ty', up_ward)  2.89 us
  transfers between devices with their start and end apart: 6, of which 4 were waited for; matrix products, arithmetic and copies ran while one was open for 3% of the time, Pallas kernels for 8%

profile of v1, /device:TPU:1, one launch (start us, length us, event | category | flops | bytes accessed | tf_op | source)
XLA Modules:
  0.0 121.7 jit_solution(5438913561254964984)
XLA Ops:
  0.6 9.4 %resample_1.1 = bf16[32,104,128]{2,1,0:T(8,128)(2,1)} custom-call(s32[64]{0:T(128)} %dest_ref.3, s32[64]{0:T(128)} %win_ref.3, s32[64]{0:T(128)} %choice_ref.3, bf16[128,64]{1,0:T(8,128)(2,1)} %bitcast.53, bf16[64,208,128]{2,1,0:T(8,128)(2,1)} %bitcast.36, bf16[8,128,128]{2,1,0:T(8,128)(2,1)} %bank_ref.3), custom_call_target="tpu_custom_call" | custom-call | flops 327155712 | bytes 20480000 | tf_op jit(solution)/shard_map/resample_1/pallas_call | solution.py:120
  10.0 7.1 %all-to-all-start.1 = ((bf16[32,104,128]{2,1,0:T(8,128)(2,1)}), bf16[32,104,128]{2,1,0:T(8,128)(2,1)S(1)}, u32[]{:S(2)}, u32[]{:S(2)}) async-start(bf16[32,104,128]{2,1,0:T(8,128)(2,1)} %resample_1.1), calls=%async_computation.1 | async-start | bytes 1703936 | tf_op jit(solution)/shard_map/all_to_all | solution.py:482
  17.2 9.4 %resample_0.1 = bf16[32,112,128]{2,1,0:T(8,128)(2,1)} custom-call(s32[64]{0:T(128)} %dest_ref.3, s32[64]{0:T(128)} %win_ref.3, s32[64]{0:T(128)} %choice_ref.3, bf16[128,64]{1,0:T(8,128)(2,1)} %bitcast.54, bf16[64,208,128]{2,1,0:T(8,128)(2,1)} %bitcast.37, bf16[8,128,128]{2,1,0:T(8,128)(2,1)} %bank_ref.3), custom_call_target="tpu_custom_call" | custom-call | flops 327155712 | bytes 20480000 | tf_op jit(solution)/shard_map/resample_0/pallas_call | solution.py:120
  26.6 0.0 copy-start.8
  26.6 13.4 %all-to-all-done.1.got1_ref = bf16[32,104,128]{2,1,0:T(8,128)(2,1)S(1)} async-done(((bf16[32,104,128]{2,1,0:T(8,128)(2,1)}), bf16[32,104,128]{2,1,0:T(8,128)(2,1)S(1)}, u32[]{:S(2)}, u32[]{:S(2)}) %all-to-all-start.1) | async-done | bytes 852000 | tf_op jit(solution)/shard_map/all_to_all | solution.py:482
  40.0 3.1 %all-to-all-start = ((bf16[32,112,128]{2,1,0:T(8,128)(2,1)}), bf16[32,112,128]{2,1,0:T(8,128)(2,1)S(1)}, u32[]{:S(2)}, u32[]{:S(2)}) async-start(bf16[32,112,128]{2,1,0:T(8,128)(2,1)} %resample_0.1), calls=%async_computation | async-start | bytes 1835008 | tf_op jit(solution)/shard_map/all_to_all | solution.py:482
  43.1 0.0 copy-start.3
  43.1 0.2 pad_bitcast_fusion
  43.5 0.6 copy-done.3
  44.0 0.7 copy.25
  44.7 1.2 concatenate.14.one_ref
  45.9 21.5 %all-to-all-done.got0_ref = bf16[32,112,128]{2,1,0:T(8,128)(2,1)S(1)} async-done(((bf16[32,112,128]{2,1,0:T(8,128)(2,1)}), bf16[32,112,128]{2,1,0:T(8,128)(2,1)S(1)}, u32[]{:S(2)}, u32[]{:S(2)}) %all-to-all-start) | async-done | bytes 917536 | tf_op jit(solution)/shard_map/all_to_all | solution.py:482
  67.4 0.9 copy-done
  68.3 6.1 %grid.1 = (bf16[13,256,128]{2,1,0:T(8,128)(2,1)}, bf16[4096,128]{1,0:T(8,128)(2,1)}, bf16[512,128]{1,0:T(8,128)(2,1)}, bf16[512,128]{1,0:T(8,128)(2,1)}) custom-call(bf16[32,112,128]{2,1,0:T(8,128)(2,1)} %copy-done, bf16[32,104,128]{2,1,0:T(8,128)(2,1)} %copy-done.1, bf16[160,128]{1,0:T(8,128)(2,1)} %constant.7.clone.perm_ref), custom_call_target="tpu_custom_call" | custom-call | tf_op jit(solution)/shard_map/grid/pallas_call | solution.py:221
  74.5 2.9 %collective-permute-start = (bf16[512,128]{1,0:T(8,128)(2,1)}, bf16[512,128]{1,0:T(8,128)(2,1)S(1)}, u32[]{:S(2)}, u32[]{:S(2)}) collective-permute-start(bf16[512,128]{1,0:T(8,128)(2,1)} %get-tuple-element.8), channel_id=1, source_target_pairs={{0,8},{8,16},{16,24},{1,9},{9,17},{17,25},{2,10},{10,18},{18,26},{... | collective-permute-start | bytes 393224 | tf_op jit(solution)/shard_map/ppermute | solution.py:249
  77.4 1.9 %collective-permute-start.1 = (bf16[512,128]{1,0:T(8,128)(2,1)}, bf16[512,128]{1,0:T(8,128)(2,1)S(1)}, u32[]{:S(2)}, u32[]{:S(2)}) collective-permute-start(bf16[512,128]{1,0:T(8,128)(2,1)} %get-tuple-element.9), channel_id=1, source_target_pairs={{8,0},{16,8},{24,16},{9,1},{17,9},{25,17},{10,2},{18,10},{26,18},{... | collective-permute-start | bytes 393224 | tf_op jit(solution)/shard_map/ppermute | solution.py:250
  79.3 0.9 fusion.3
  80.2 3.7 %collective-permute-done.1.fr_ref = bf16[512,128]{1,0:T(8,128)(2,1)S(1)} collective-permute-done((bf16[512,128]{1,0:T(8,128)(2,1)}, bf16[512,128]{1,0:T(8,128)(2,1)S(1)}, u32[]{:S(2)}, u32[]{:S(2)}) %collective-permute-start.1) | collective-permute-done | bytes 131104 | tf_op jit(solution)/shard_map/ppermute | solution.py:250
  83.9 2.3 %collective-permute-start.2 = (bf16[320,128]{1,0:T(8,128)(2,1)S(1)}, bf16[320,128]{1,0:T(8,128)(2,1)S(1)}, u32[]{:S(2)}, u32[]{:S(2)}) collective-permute-start(bf16[320,128]{1,0:T(8,128)(2,1)S(1)} %pad_maximum_fusion), channel_id=1, source_target_pairs={{0,1},{1,2},{2,3},{3,4},{4,5},{5,6},{6,7},{8,9},{9,10},{10,11},{11... | collective-permute-start | bytes 245768 | tf_op jit(solution)/shard_map/ppermute | solution.py:254
  86.3 1.3 %collective-permute-start.3 = (bf16[320,128]{1,0:T(8,128)(2,1)S(1)}, bf16[320,128]{1,0:T(8,128)(2,1)S(1)}, u32[]{:S(2)}, u32[]{:S(2)}) collective-permute-start(bf16[320,128]{1,0:T(8,128)(2,1)S(1)} %pad_maximum_fusion.1), channel_id=1, source_target_pairs={{1,0},{2,1},{3,2},{4,3},{5,4},{6,5},{7,6},{9,8},{10,9},{11,10},{12... | collective-permute-start | bytes 245768 | tf_op jit(solution)/shard_map/ppermute | solution.py:255
  87.6 1.0 fusion.2
  88.6 2.9 %collective-permute-done.3.below_ref = bf16[320,128]{1,0:T(8,128)(2,1)S(1)} collective-permute-done((bf16[320,128]{1,0:T(8,128)(2,1)S(1)}, bf16[320,128]{1,0:T(8,128)(2,1)S(1)}, u32[]{:S(2)}, u32[]{:S(2)}) %collective-permute-start.3) | collective-permute-done | bytes 81952 | tf_op jit(solution)/shard_map/ppermute | solution.py:255
  91.5 0.6 copy-done.7
  92.1 29.5 %encoder.1 = bf16[32,16,512]{2,1,0:T(8,128)(2,1)} custom-call(bf16[4096,128]{1,0:T(8,128)(2,1)} %get-tuple-element.7.main_ref, bf16[512,128]{1,0:T(8,128)(2,1)} %copy-done.4, bf16[512,128]{1,0:T(8,128)(2,1)} %copy-done.5, bf16[320,128]{1,0:T(8,128)(2,1)} %copy-done.6, bf16[320,128]{1,0:T(8,128)(2,1)} %copy-done.7, ...), custom_call_target="tpu_custom_call" | custom-call | tf_op jit(solution)/shard_map/encoder/pallas_call | solution.py:429
  (28 shorter events, 0.1 us)
Async XLA Ops:
  10.0 29.9 %all-to-all-start.1 = ((bf16[32,104,128]{2,1,0:T(8,128)(2,1)}), bf16[32,104,128]{2,1,0:T(8,128)(2,1)S(1)}, u32[]{:S(2)}, u32[]{:S(2)}) async-start(bf16[32,104,128]{2,1,0:T(8,128)(2,1)} %resample_1.1), calls=%async_computation.1 | async-start | bytes 1703936 | tf_op jit(solution)/shard_map/all_to_all | solution.py:482
  26.6 16.5 %copy-start.8 = (bf16[3,3,13,64]{3,2,1,0:T(8,128)(2,1)S(1)}, bf16[3,3,13,64]{3,2,1,0:T(8,128)(2,1)}, u32[]{:S(2)}) copy-start(bf16[3,3,13,64]{3,2,1,0:T(8,128)(2,1)} %param.21) | copy-start | bytes 44932
  40.0 3.4 %copy-start.1 = (bf16[32,104,128]{2,1,0:T(8,128)(2,1)}, bf16[32,104,128]{2,1,0:T(8,128)(2,1)S(1)}, u32[]{:S(2)}) copy-start(bf16[32,104,128]{2,1,0:T(8,128)(2,1)S(1)} %all-to-all-done.1.got1_ref) | copy-start | bytes 2555908
  40.0 27.4 %all-to-all-start = ((bf16[32,112,128]{2,1,0:T(8,128)(2,1)}), bf16[32,112,128]{2,1,0:T(8,128)(2,1)S(1)}, u32[]{:S(2)}, u32[]{:S(2)}) async-start(bf16[32,112,128]{2,1,0:T(8,128)(2,1)} %resample_0.1), calls=%async_computation | async-start | bytes 1835008 | tf_op jit(solution)/shard_map/all_to_all | solution.py:482
  43.1 1.0 copy-start.3
  45.9 41.7 %copy-start.2 = (bf16[3,3,128,128]{3,2,1,0:T(8,128)(2,1)S(1)}, bf16[3,3,128,128]{3,2,1,0:T(8,128)(2,1)}, u32[]{:S(2)}) copy-start(bf16[3,3,128,128]{3,2,1,0:T(8,128)(2,1)} %param.23) | copy-start | bytes 884740
  67.4 0.9 copy-start
  74.5 9.4 %collective-permute-start = (bf16[512,128]{1,0:T(8,128)(2,1)}, bf16[512,128]{1,0:T(8,128)(2,1)S(1)}, u32[]{:S(2)}, u32[]{:S(2)}) collective-permute-start(bf16[512,128]{1,0:T(8,128)(2,1)} %get-tuple-element.8), channel_id=1, source_target_pairs={{0,8},{8,16},{16,24},{1,9},{9,17},{17,25},{2,10},{10,18},{18,26},{... | collective-permute-start | bytes 393224 | tf_op jit(solution)/shard_map/ppermute | solution.py:249
  77.4 6.5 %collective-permute-start.1 = (bf16[512,128]{1,0:T(8,128)(2,1)}, bf16[512,128]{1,0:T(8,128)(2,1)S(1)}, u32[]{:S(2)}, u32[]{:S(2)}) collective-permute-start(bf16[512,128]{1,0:T(8,128)(2,1)} %get-tuple-element.9), channel_id=1, source_target_pairs={{8,0},{16,8},{24,16},{9,1},{17,9},{25,17},{10,2},{18,10},{26,18},{... | collective-permute-start | bytes 393224 | tf_op jit(solution)/shard_map/ppermute | solution.py:250
  83.9 7.6 %copy-start.5 = (bf16[512,128]{1,0:T(8,128)(2,1)}, bf16[512,128]{1,0:T(8,128)(2,1)S(1)}, u32[]{:S(2)}) copy-start(bf16[512,128]{1,0:T(8,128)(2,1)S(1)} %collective-permute-done.1.fr_ref) | copy-start | bytes 393220
  83.9 7.6 %copy-start.4 = (bf16[512,128]{1,0:T(8,128)(2,1)}, bf16[512,128]{1,0:T(8,128)(2,1)S(1)}, u32[]{:S(2)}) copy-start(bf16[512,128]{1,0:T(8,128)(2,1)S(1)} %collective-permute-done.fl_ref) | copy-start | bytes 393220
  83.9 4.7 %collective-permute-start.2 = (bf16[320,128]{1,0:T(8,128)(2,1)S(1)}, bf16[320,128]{1,0:T(8,128)(2,1)S(1)}, u32[]{:S(2)}, u32[]{:S(2)}) collective-permute-start(bf16[320,128]{1,0:T(8,128)(2,1)S(1)} %pad_maximum_fusion), channel_id=1, source_target_pairs={{0,1},{1,2},{2,3},{3,4},{4,5},{5,6},{6,7},{8,9},{9,10},{10,11},{11... | collective-permute-start | bytes 245768 | tf_op jit(solution)/shard_map/ppermute | solution.py:254
  86.3 5.2 %collective-permute-start.3 = (bf16[320,128]{1,0:T(8,128)(2,1)S(1)}, bf16[320,128]{1,0:T(8,128)(2,1)S(1)}, u32[]{:S(2)}, u32[]{:S(2)}) collective-permute-start(bf16[320,128]{1,0:T(8,128)(2,1)S(1)} %pad_maximum_fusion.1), channel_id=1, source_target_pairs={{1,0},{2,1},{3,2},{4,3},{5,4},{6,5},{7,6},{9,8},{10,9},{11,10},{12... | collective-permute-start | bytes 245768 | tf_op jit(solution)/shard_map/ppermute | solution.py:255
  88.6 2.9 %copy-start.6 = (bf16[320,128]{1,0:T(8,128)(2,1)}, bf16[320,128]{1,0:T(8,128)(2,1)S(1)}, u32[]{:S(2)}) copy-start(bf16[320,128]{1,0:T(8,128)(2,1)S(1)} %collective-permute-done.2.above_ref) | copy-start | bytes 245764
  91.5 0.6 copy-start.7
